TPU v7x, 32 devices: a whole 2x2x4 slice. The times are simulated.
32 devices in a mesh: wide: 8 (over z, x), tensor: 4 (over y, core).
Axes of the slice: x: 2, y: 2, z: 4, core: 2. Of those that a mesh axis runs over, the one named last changes fastest.
Arguments:
- tokens: bfloat16 [16, 1024, 768], P('wide', 'tensor'), may hold values from -6 to 6
- cotangent: bfloat16 [16, 1024, 768], P('wide', 'tensor'), may hold values from -6 to 6
- ln1_gain: bfloat16 [2, 768], P(None, 'wide'), may hold values from 0.25 to 1.75
- ln1_bias: bfloat16 [2, 768], P(None, 'wide'), may hold values from -3 to 3
- ln2_gain: bfloat16 [2, 768], P(None, 'wide'), may hold values from 0.25 to 1.75
- ln2_bias: bfloat16 [2, 768], P(None, 'wide'), may hold values from -3 to 3
- qkv_weight: bfloat16 [2, 3, 768, 768], P(None, None, 'wide', 'tensor'), may hold values from -0.21875 to 0.21875
- qkv_bias: bfloat16 [2, 3, 12, 64], P(None, None, 'tensor', 'wide'), may hold values from -3 to 3
- dense_weight: bfloat16 [2, 768, 768], P(None, 'tensor', 'wide'), may hold values from -1.75 to 1.75
- dense_bias: bfloat16 [2, 768], P(None, 'wide'), may hold values from -3 to 3
- fc1_weight: bfloat16 [2, 768, 3072], P(None, 'wide', 'tensor'), may hold values from -0.21875 to 0.21875
- fc1_bias: bfloat16 [2, 12, 256], P(None, 'tensor', 'wide'), may hold values from -3 to 3
- fc2_weight: bfloat16 [2, 3072, 768], P(None, 'tensor', 'wide'), may hold values from -0.109375 to 0.109375
- fc2_bias: bfloat16 [2, 768], P(None, 'wide'), may hold values from -3 to 3
Outputs:
- mixed: bfloat16 [16, 1024, 768], P('wide', 'tensor')
- input_grad: bfloat16 [16, 1024, 768], P('wide', 'tensor')
- ln1_gain_grad: float32 [2, 768], P(None, 'wide')
- ln1_bias_grad: float32 [2, 768], P(None, 'wide')
- ln2_gain_grad: float32 [2, 768], P(None, 'wide')
- ln2_bias_grad: float32 [2, 768], P(None, 'wide')
- qkv_weight_grad: float32 [2, 3, 768, 768], P(None, None, 'wide', 'tensor')
- qkv_bias_grad: float32 [2, 3, 12, 64], P(None, None, 'tensor', 'wide')
- dense_weight_grad: float32 [2, 768, 768], P(None, 'tensor', 'wide')
- dense_bias_grad: float32 [2, 768], P(None, 'wide')
- fc1_weight_grad: float32 [2, 768, 3072], P(None, 'wide', 'tensor')
- fc1_bias_grad: float32 [2, 12, 256], P(None, 'tensor', 'wide')
- fc2_weight_grad: float32 [2, 3072, 768], P(None, 'tensor', 'wide')
- fc2_bias_grad: float32 [2, 768], P(None, 'wide')
All inputs are finite; a program needn't handle non-finite values.
Results may differ from a plain program's by a relative error of at most 0.018.
Values may be sent and summed in bfloat16 or wider, within the bound.
A program may use at most 256 MiB of HBM per device.

v0:
```python
from functools import partial
import math

import jax
import jax.numpy as jnp
from jax import lax
from jax.sharding import PartitionSpec as P

HD = 64
ROT = 16


EPSILON = 1e-05
BLOCK_ROWS = 512


def rotary_tables(seq_len):
    half_rot = ROT // 2
    positions = jnp.arange(seq_len, dtype=jnp.float32)
    freq_index = jnp.arange(half_rot, dtype=jnp.float32)
    inverse = jnp.exp(freq_index * (-2.0 * math.log(10000.0) / ROT))
    angles = positions[:, None] * inverse[None, :]
    return (jnp.cos(angles)[:, None, :], jnp.sin(angles)[:, None, :])


def rotate(values, cos_tab, sin_tab):
    half_rot = ROT // 2
    front_half = values[..., :half_rot]
    second = values[..., half_rot:ROT]
    return jnp.concatenate(
        [
            front_half * cos_tab - second * sin_tab,
            second * cos_tab + front_half * sin_tab,
            values[..., ROT:],
        ],
        axis=-1,
    )


def unrotate(grads_in, cos_tab, sin_tab):
    half_rot = ROT // 2
    front_half = grads_in[..., :half_rot]
    second = grads_in[..., half_rot:ROT]
    return jnp.concatenate(
        [
            front_half * cos_tab + second * sin_tab,
            second * cos_tab - front_half * sin_tab,
            grads_in[..., ROT:],
        ],
        axis=-1,
    )


def normalize_rows(residual):
    mean_val = jnp.mean(residual, axis=-1, keepdims=True)
    centered = residual - mean_val
    variance = jnp.mean(centered * centered, axis=-1, keepdims=True)
    inv_std = lax.rsqrt(variance + EPSILON)
    return (centered * inv_std, inv_std)


def norm_backward(grad_norm, scaled, inv_std, gain_vec):
    scaled_grad = grad_norm * gain_vec
    mean_grad = jnp.mean(scaled_grad, axis=-1, keepdims=True)
    mean_cross = jnp.mean(scaled_grad * scaled, axis=-1, keepdims=True)
    return inv_std * (scaled_grad - mean_grad - scaled * mean_cross)


def mask_scores(scores, row_start, row_end):
    query_pos = row_start + jnp.arange(row_end - row_start)[:, None]
    key_pos = jnp.arange(row_end)[None, :]
    return jnp.where(key_pos <= query_pos, scores, -1e30)


def attend_forward(queries, key_rows, value_rows, score_scale):
    seq_len = queries.shape[1]
    block_len = min(BLOCK_ROWS, seq_len)
    outputs = []
    lse_parts = []
    for block_idx in range(seq_len // block_len):
        row_start = block_idx * block_len
        row_end = row_start + block_len
        scores = (
            jnp.einsum(
                "sqhe,skhe->shqk",
                queries[:, row_start:row_end],
                key_rows[:, :row_end],
                preferred_element_type=jnp.float32,
            )
            * score_scale
        )
        scores = mask_scores(scores, row_start, row_end)
        row_peak = jnp.max(scores, axis=-1, keepdims=True)
        exp_scores = jnp.exp(scores - row_peak)
        row_total = jnp.sum(exp_scores, axis=-1, keepdims=True)
        prob_rows = exp_scores / row_total
        outputs.append(
            jnp.einsum(
                "shqk,skhe->sqhe",
                prob_rows.astype(jnp.bfloat16),
                value_rows[:, :row_end],
                preferred_element_type=jnp.float32,
            )
        )
        lse_parts.append(row_peak + jnp.log(row_total))
    return (jnp.concatenate(outputs, axis=1), jnp.concatenate(lse_parts, axis=2))


def attend_backward(queries, key_rows, value_rows, grad_heads, log_totals, score_scale):
    seq_len = queries.shape[1]
    block_len = min(BLOCK_ROWS, seq_len)
    grad_q_parts = []
    grad_k = jnp.zeros(key_rows.shape, jnp.float32)
    grad_v = jnp.zeros(value_rows.shape, jnp.float32)
    for block_idx in range(seq_len // block_len):
        row_start = block_idx * block_len
        row_end = row_start + block_len
        query_block = queries[:, row_start:row_end]
        grad_block = grad_heads[:, row_start:row_end]
        scores = (
            jnp.einsum(
                "sqhe,skhe->shqk",
                query_block,
                key_rows[:, :row_end],
                preferred_element_type=jnp.float32,
            )
            * score_scale
        )
        scores = mask_scores(scores, row_start, row_end)
        prob_rows = jnp.exp(scores - log_totals[:, :, row_start:row_end])
        grad_probs = jnp.einsum(
            "sqhe,skhe->shqk",
            grad_block,
            value_rows[:, :row_end],
            preferred_element_type=jnp.float32,
        )
        row_delta = jnp.sum(prob_rows * grad_probs, axis=-1, keepdims=True)
        grad_scores = (prob_rows * (grad_probs - row_delta)).astype(jnp.bfloat16)
        grad_q_parts.append(
            jnp.einsum(
                "shqk,skhe->sqhe",
                grad_scores,
                key_rows[:, :row_end],
                preferred_element_type=jnp.float32,
            )
            * score_scale
        )
        grad_k = grad_k.at[:, :row_end].add(
            jnp.einsum(
                "shqk,sqhe->skhe", grad_scores, query_block, preferred_element_type=jnp.float32
            )
            * score_scale
        )
        grad_v = grad_v.at[:, :row_end].add(
            jnp.einsum(
                "shqk,sqhe->skhe",
                prob_rows.astype(jnp.bfloat16),
                grad_block,
                preferred_element_type=jnp.float32,
            )
        )
    return (jnp.concatenate(grad_q_parts, axis=1), grad_k, grad_v)


def unpack(gathered):
    (
        gain_a,
        shift_a,
        gain_b,
        shift_b,
        query_key_value_weight,
        query_key_value_bias,
        output_weight,
        out_b,
        up_weight,
        up_bias,
        down_weight,
        down_b,
    ) = gathered
    return (
        gain_a,
        shift_a,
        gain_b,
        shift_b,
        query_key_value_weight,
        query_key_value_bias.reshape(3, -1),
        output_weight,
        out_b,
        up_weight,
        up_bias.reshape(-1),
        down_weight,
        down_b,
    )


def fetch_layer(shards, layer_idx):
    (
        gain_a,
        shift_a,
        gain_b,
        shift_b,
        query_key_value_weight,
        query_key_value_bias,
        output_weight,
        out_b,
        up_weight,
        up_bias,
        down_weight,
        down_b,
    ) = shards
    return unpack(
        (
            lax.all_gather(gain_a[layer_idx], "wide", axis=0, tiled=True),
            lax.all_gather(shift_a[layer_idx], "wide", axis=0, tiled=True),
            lax.all_gather(gain_b[layer_idx], "wide", axis=0, tiled=True),
            lax.all_gather(shift_b[layer_idx], "wide", axis=0, tiled=True),
            lax.all_gather(query_key_value_weight[layer_idx], "wide", axis=1, tiled=True),
            lax.all_gather(query_key_value_bias[layer_idx], "wide", axis=2, tiled=True),
            lax.all_gather(output_weight[layer_idx], "wide", axis=1, tiled=True),
            lax.all_gather(out_b[layer_idx], "wide", axis=0, tiled=True),
            lax.all_gather(up_weight[layer_idx], "wide", axis=0, tiled=True),
            lax.all_gather(up_bias[layer_idx], "wide", axis=1, tiled=True),
            lax.all_gather(down_weight[layer_idx], "wide", axis=1, tiled=True),
            lax.all_gather(down_b[layer_idx], "wide", axis=0, tiled=True),
        )
    )


def fetch_again(shards, layer_idx):
    (
        gain_a,
        shift_a,
        gain_b,
        shift_b,
        query_key_value_weight,
        query_key_value_bias,
        output_weight,
        out_b,
        up_weight,
        up_bias,
        down_weight,
        down_b,
    ) = shards
    return unpack(
        (
            lax.all_gather(gain_a[layer_idx], "wide", axis=0, tiled=True),
            lax.all_gather(shift_a[layer_idx], "wide", axis=0, tiled=True),
            lax.all_gather(gain_b[layer_idx], "wide", axis=0, tiled=True),
            lax.all_gather(shift_b[layer_idx], "wide", axis=0, tiled=True),
            lax.all_gather(query_key_value_weight[layer_idx], "wide", axis=1, tiled=True),
            lax.all_gather(query_key_value_bias[layer_idx], "wide", axis=2, tiled=True),
            lax.all_gather(output_weight[layer_idx], "wide", axis=1, tiled=True),
            lax.all_gather(out_b[layer_idx], "wide", axis=0, tiled=True),
            lax.all_gather(up_weight[layer_idx], "wide", axis=0, tiled=True),
            lax.all_gather(up_bias[layer_idx], "wide", axis=1, tiled=True),
            lax.all_gather(down_weight[layer_idx], "wide", axis=1, tiled=True),
            lax.all_gather(down_b[layer_idx], "wide", axis=0, tiled=True),
        )
    )


def body(
    tokens,
    cotangent,
    ln1_gain,
    ln1_bias,
    ln2_gain,
    ln2_bias,
    qkv_weight,
    qkv_bias,
    dense_weight,
    dense_bias,
    fc1_weight,
    fc1_bias,
    fc2_weight,
    fc2_bias,
):
    shards = (
        ln1_gain,
        ln1_bias,
        ln2_gain,
        ln2_bias,
        qkv_weight,
        qkv_bias,
        dense_weight,
        dense_bias,
        fc1_weight,
        fc1_bias,
        fc2_weight,
        fc2_bias,
    )
    layers_n = qkv_weight.shape[0]
    seqs_n = tokens.shape[0]
    seq_len = tokens.shape[1] * lax.axis_size("tensor")
    heads_local = qkv_bias.shape[2]
    groups_local = fc1_bias.shape[1]
    cos_tab, sin_tab = rotary_tables(seq_len)
    score_scale = 1.0 / math.sqrt(HD)
    residual = tokens.astype(jnp.float32)
    saved_acts = []
    kept_weights = []
    for layer_idx in range(layers_n):
        weights_now = fetch_layer(shards, layer_idx)
        kept_weights.append(weights_now)
        (
            gain_a,
            shift_a,
            gain_b,
            shift_b,
            query_key_value_weight,
            query_key_value_bias,
            output_weight,
            out_b,
            up_weight,
            up_bias,
            down_weight,
            down_b,
        ) = weights_now
        scaled, inv_std = normalize_rows(residual)
        first_norm_rows = (scaled * gain_a + shift_a).astype(jnp.bfloat16)
        second_norm_rows = (scaled * gain_b + shift_b).astype(jnp.bfloat16)
        full_input_first, full_input_second = (
            lax.all_gather(first_norm_rows, "tensor", axis=1, tiled=True),
            lax.all_gather(second_norm_rows, "tensor", axis=1, tiled=True),
        )
        linear_rows = (
            jnp.einsum(
                "ahf,gft->gaht",
                full_input_first,
                query_key_value_weight,
                preferred_element_type=jnp.float32,
            )
            + query_key_value_bias[:, None, None, :]
        )
        linear_rows = linear_rows.reshape(3, seqs_n, seq_len, heads_local, HD)
        queries = rotate(linear_rows[0], cos_tab, sin_tab).astype(jnp.bfloat16)
        key_rows = rotate(linear_rows[1], cos_tab, sin_tab).astype(jnp.bfloat16)
        value_rows = linear_rows[2].astype(jnp.bfloat16)
        head_output_rows, log_totals = attend_forward(queries, key_rows, value_rows, score_scale)
        head_output_rows = head_output_rows.reshape(seqs_n, seq_len, heads_local * HD).astype(
            jnp.bfloat16
        )
        hidden_rows = (
            jnp.einsum(
                "kwc,ci->kwi", full_input_second, up_weight, preferred_element_type=jnp.float32
            )
            + up_bias
        )
        activated_hidden = jax.nn.gelu(hidden_rows, approximate=False).astype(jnp.bfloat16)
        partial_sum = jnp.einsum(
            "bwk,kx->bwx", head_output_rows, output_weight, preferred_element_type=jnp.float32
        ) + jnp.einsum(
            "prc,ck->prk", activated_hidden, down_weight, preferred_element_type=jnp.float32
        )
        branch_output = lax.psum_scatter(
            partial_sum.astype(jnp.bfloat16), "tensor", scatter_dimension=1, tiled=True
        ).astype(jnp.float32)
        saved_acts.append(
            (
                scaled,
                inv_std,
                full_input_first,
                full_input_second,
                queries,
                key_rows,
                value_rows,
                log_totals,
                head_output_rows,
                hidden_rows,
                activated_hidden,
            )
        )
        residual = residual + branch_output + out_b + down_b
    mixed = residual.astype(jnp.bfloat16)
    grad_resid = cotangent.astype(jnp.float32)
    summed_grads = [None] * layers_n
    for layer_idx in reversed(range(layers_n)):
        (
            scaled,
            inv_std,
            full_input_first,
            full_input_second,
            queries,
            key_rows,
            value_rows,
            log_totals,
            head_output_rows,
            hidden_rows,
            activated_hidden,
        ) = saved_acts[layer_idx]
        weights_now = fetch_again(shards, layer_idx)
        (
            gain_a,
            shift_a,
            gain_b,
            shift_b,
            query_key_value_weight,
            query_key_value_bias,
            output_weight,
            out_b,
            up_weight,
            up_bias,
            down_weight,
            down_b,
        ) = weights_now
        bias_sum = jnp.sum(grad_resid, axis=(0, 1))
        full_gradient = lax.all_gather(
            grad_resid.astype(jnp.bfloat16), "tensor", axis=1, tiled=True
        )
        out_w_grad = jnp.einsum(
            "boq,bof->qf", head_output_rows, full_gradient, preferred_element_type=jnp.float32
        )
        down_w_grad = jnp.einsum(
            "eca,ech->ah", activated_hidden, full_gradient, preferred_element_type=jnp.float32
        )
        grad_active = jnp.einsum(
            "qky,ay->qka", full_gradient, down_weight, preferred_element_type=jnp.float32
        )
        gelu_value, gelu_pull = jax.vjp(partial(jax.nn.gelu, approximate=False), hidden_rows)
        hidden_gradient = gelu_pull(grad_active)[0].astype(jnp.bfloat16)
        up_w_grad = jnp.einsum(
            "rae,rak->ek", full_input_second, hidden_gradient, preferred_element_type=jnp.float32
        )
        up_b_grad = jnp.sum(hidden_gradient, axis=(0, 1), dtype=jnp.float32).reshape(
            groups_local, -1
        )
        grad_norm_b = jnp.einsum(
            "xzt,ot->xzo", hidden_gradient, up_weight, preferred_element_type=jnp.float32
        )
        grad_heads = jnp.einsum(
            "gbn,yn->gby", full_gradient, output_weight, preferred_element_type=jnp.float32
        ).astype(jnp.bfloat16)
        grad_heads = grad_heads.reshape(seqs_n, seq_len, heads_local, HD)
        grad_q, grad_k, grad_v = attend_backward(
            queries, key_rows, value_rows, grad_heads, log_totals, score_scale
        )
        linear_gradient = jnp.stack(
            [unrotate(grad_q, cos_tab, sin_tab), unrotate(grad_k, cos_tab, sin_tab), grad_v]
        ).astype(jnp.bfloat16)
        linear_gradient = linear_gradient.reshape(3, seqs_n, seq_len, heads_local * HD)
        qkv_w_grad = jnp.einsum(
            "qif,vqih->vfh", full_input_first, linear_gradient, preferred_element_type=jnp.float32
        )
        qkv_b_grad = jnp.sum(linear_gradient, axis=(1, 2), dtype=jnp.float32).reshape(
            3, heads_local, HD
        )
        grad_norm_a = jnp.einsum(
            "abqu,awu->bqw",
            linear_gradient,
            query_key_value_weight,
            preferred_element_type=jnp.float32,
        )
        local_a, local_b = (
            lax.psum_scatter(
                grad_norm_a.astype(jnp.bfloat16), "tensor", scatter_dimension=1, tiled=True
            ).astype(jnp.float32),
            lax.psum_scatter(
                grad_norm_b.astype(jnp.bfloat16), "tensor", scatter_dimension=1, tiled=True
            ).astype(jnp.float32),
        )
        gain_a_part = jnp.sum(local_a * scaled, axis=(0, 1))
        shift_a_part = jnp.sum(local_a, axis=(0, 1))
        gain_b_part = jnp.sum(local_b * scaled, axis=(0, 1))
        shift_b_part = jnp.sum(local_b, axis=(0, 1))
        through_norms = norm_backward(local_a, scaled, inv_std, gain_a) + norm_backward(
            local_b, scaled, inv_std, gain_b
        )
        small_sums = lax.psum(
            (gain_a_part, shift_a_part, gain_b_part, shift_b_part, bias_sum), "tensor"
        )
        grad_resid = grad_resid + through_norms
        members = (
            small_sums[0],
            small_sums[1],
            small_sums[2],
            small_sums[3],
            qkv_w_grad,
            qkv_b_grad,
            out_w_grad,
            small_sums[4],
            up_w_grad,
            up_b_grad,
            down_w_grad,
        )
        summed_grads[layer_idx] = (
            lax.psum_scatter(members[0], "wide", scatter_dimension=0, tiled=True),
            lax.psum_scatter(members[1], "wide", scatter_dimension=0, tiled=True),
            lax.psum_scatter(members[2], "wide", scatter_dimension=0, tiled=True),
            lax.psum_scatter(members[3], "wide", scatter_dimension=0, tiled=True),
            lax.psum_scatter(members[4], "wide", scatter_dimension=1, tiled=True),
            lax.psum_scatter(members[5], "wide", scatter_dimension=2, tiled=True),
            lax.psum_scatter(members[6], "wide", scatter_dimension=1, tiled=True),
            lax.psum_scatter(members[7], "wide", scatter_dimension=0, tiled=True),
            lax.psum_scatter(members[8], "wide", scatter_dimension=0, tiled=True),
            lax.psum_scatter(members[9], "wide", scatter_dimension=1, tiled=True),
            lax.psum_scatter(members[10], "wide", scatter_dimension=1, tiled=True),
        )
    input_grad = grad_resid.astype(jnp.bfloat16)
    stacked = [
        jnp.stack([summed_grads[layer_idx][member_idx] for layer_idx in range(layers_n)])
        for member_idx in range(11)
    ]
    return (
        mixed,
        input_grad,
        stacked[0],
        stacked[1],
        stacked[2],
        stacked[3],
        stacked[4],
        stacked[5],
        stacked[6],
        stacked[7],
        stacked[8],
        stacked[9],
        stacked[10],
        stacked[7],
    )


def solution(mesh):
    return jax.shard_map(
        body,
        mesh=mesh,
        in_specs=(
            P("wide", "tensor", None),
            P("wide", "tensor", None),
            P(None, "wide"),
            P(None, "wide"),
            P(None, "wide"),
            P(None, "wide"),
            P(None, None, "wide", "tensor"),
            P(None, None, "tensor", "wide"),
            P(None, "tensor", "wide"),
            P(None, "wide"),
            P(None, "wide", "tensor"),
            P(None, "tensor", "wide"),
            P(None, "tensor", "wide"),
            P(None, "wide"),
        ),
        out_specs=(
            P("wide", "tensor", None),
            P("wide", "tensor", None),
            P(None, "wide"),
            P(None, "wide"),
            P(None, "wide"),
            P(None, "wide"),
            P(None, None, "wide", "tensor"),
            P(None, None, "tensor", "wide"),
            P(None, "tensor", "wide"),
            P(None, "wide"),
            P(None, "wide", "tensor"),
            P(None, "tensor", "wide"),
            P(None, "tensor", "wide"),
            P(None, "wide"),
        ),
        check_vma=False,
    )
```

profile of v0, /device:TPU:0, one launch (start us, length us, event | category | flops | bytes accessed | tf_op | source)
XLA Modules:
  0.0 1475.1 jit_solution(830028967497261899)
XLA Ops:
  19.1 39.4 %all-reduce.30 = (bf16[768]{0:T(1024)(128)(2,1)S(1)}, bf16[768]{0:T(1024)(128)(2,1)S(1)}, bf16[768]{0:T(1024)(128)(2,1)S(1)}, bf16[768]{0:T(1024)(128)(2,1)S(1)}...) all-reduce(bf16[768]{0:T(1024)(128)(2,1)S(1)} %dynamic-update-slice, ...), channel_id=20, replica_groups=mesh['wide'=8,'tensor'=4] {'wide'}, use_global_device_ids=true, to_apply=%add.13 | all-reduce | flops 9216 | bytes 36864
  64.9 30.5 %all-gather.3 = bf16[1,3,3,64]{2,1,0,3:T(4,128)(2,1)S(1)} all-gather(bf16[1,3,3,8]{2,1,0,3:T(4,128)(2,1)S(1)} %copy.193), channel_id=5, replica_groups=mesh['wide'=8,'tensor'=4] {'wide'}, dimensions={3}, use_global_device_ids=true | all-gather | bytes 1296 | tf_op jit(solution)/shard_map/all_gather | solution.py:218
  96.0 30.9 %all-gather.8 = bf16[1,3,256]{1,0,2:T(2,128)(2,1)S(1)} all-gather(bf16[1,3,32]{1,0,2:T(2,128)(2,1)S(1)} %copy.195), channel_id=10, replica_groups=mesh['wide'=8,'tensor'=4] {'wide'}, dimensions={2}, use_global_device_ids=true | all-gather | bytes 1728 | tf_op jit(solution)/shard_map/all_gather | solution.py:222
  128.4 32.7 %all-gather.4 = bf16[1,192,768]{1,0,2:T(2,128)(2,1)S(1)} all-gather(bf16[1,192,96]{1,0,2:T(2,128)(2,1)S(1)} %copy.194), channel_id=6, replica_groups=mesh['wide'=8,'tensor'=4] {'wide'}, dimensions={2}, use_global_device_ids=true | all-gather | bytes 331776 | tf_op jit(solution)/shard_map/all_gather | solution.py:219
  161.6 34.8 %all-gather.2 = bf16[1,3,768,192]{3,1,0,2:T(4,128)(2,1)S(1)} all-gather(bf16[1,3,96,192]{3,1,0,2:T(4,128)(2,1)S(1)} %copy.192), channel_id=4, replica_groups=mesh['wide'=8,'tensor'=4] {'wide'}, dimensions={2}, use_global_device_ids=true | all-gather | bytes 995328 | tf_op jit(solution)/shard_map/all_gather | solution.py:217
  220.5 16.0 %multiply_convert_fusion.5 = (bf16[2,1024,768]{2,1,0:T(8,128)(2,1)}, f32[2,1024,768]{2,1,0:T(8,128)}) fusion(f32[2,1024,768]{2,1,0:T(8,128)S(1)} %get-tuple-element.325, f32[768]{0:T(1024)S(1)} %reshape.573, u8[1024,768]{1,0:T(8,128)(4,1)S(1)} %get-tuple-element.201, u8[1024,768]{1,0:T(8,128)(4,1)S(1)} %get-tuple-element.200), kind=kLoop, calls=%fused_computation.63 | loop fusion | flops 111673344 | bytes 17304576 | tf_op jit(solution)/shard_map/convert_element_type | solution.py:349
  252.2 35.3 %reduce-scatter.31.cloned.1.call-done = bf16[2,256,768]{2,1,0:T(8,128)(2,1)} async-done(((bf16[2,1024,768]{2,1,0:T(8,128)(2,1)}), bf16[2,256,768]{2,1,0:T(8,128)(2,1)}) %reduce-scatter.31.cloned.1.call-update) | async-done | bytes 786448 | tf_op jit(solution)/shard_map/reduce_scatter | solution.py:355
  294.3 30.6 %all-gather.15 = bf16[1,3,3,64]{2,1,0,3:T(4,128)(2,1)S(1)} all-gather(bf16[1,3,3,8]{2,1,0,3:T(4,128)(2,1)S(1)} %copy.197), channel_id=17, replica_groups=mesh['wide'=8,'tensor'=4] {'wide'}, dimensions={3}, use_global_device_ids=true | all-gather | bytes 1296 | tf_op jit(solution)/shard_map/all_gather | solution.py:218
  325.2 31.0 %all-gather.20 = bf16[1,3,256]{1,0,2:T(2,128)(2,1)S(1)} all-gather(bf16[1,3,32]{1,0,2:T(2,128)(2,1)S(1)} %copy.199), channel_id=22, replica_groups=mesh['wide'=8,'tensor'=4] {'wide'}, dimensions={2}, use_global_device_ids=true | all-gather | bytes 1728 | tf_op jit(solution)/shard_map/all_gather | solution.py:222
  356.5 32.7 %all-gather.16 = bf16[1,192,768]{1,0,2:T(2,128)(2,1)S(1)} all-gather(bf16[1,192,96]{1,0,2:T(2,128)(2,1)S(1)} %copy.198), channel_id=18, replica_groups=mesh['wide'=8,'tensor'=4] {'wide'}, dimensions={2}, use_global_device_ids=true | all-gather | bytes 331776 | tf_op jit(solution)/shard_map/all_gather | solution.py:219
  389.7 34.8 %all-gather.14 = bf16[1,3,768,192]{3,1,0,2:T(4,128)(2,1)S(1)} all-gather(bf16[1,3,96,192]{3,1,0,2:T(4,128)(2,1)S(1)} %copy.196), channel_id=16, replica_groups=mesh['wide'=8,'tensor'=4] {'wide'}, dimensions={2}, use_global_device_ids=true | all-gather | bytes 995328 | tf_op jit(solution)/shard_map/all_gather | solution.py:217
  439.3 15.7 %multiply_convert_fusion.4 = (bf16[2,1024,768]{2,1,0:T(8,128)(2,1)}, f32[2,1024,768]{2,1,0:T(8,128)}) fusion(f32[2,1024,768]{2,1,0:T(8,128)S(1)} %get-tuple-element.330, f32[768]{0:T(1024)S(1)} %reshape.575, u8[1024,768]{1,0:T(8,128)(4,1)S(1)} %get-tuple-element.199, u8[1024,768]{1,0:T(8,128)(4,1)S(1)} %get-tuple-element.198), kind=kLoop, calls=%fused_computation.46 | loop fusion | flops 111673344 | bytes 17304576 | tf_op jit(solution)/shard_map/convert_element_type | solution.py:349
  472.2 11.1 convert_reduce_fusion
  489.1 8.6 fusion.1
  545.8 7.2 fusion.124
  559.2 18.5 %reduce-scatter.35.cloned.1.call-done = bf16[2,256,768]{2,1,0:T(8,128)(2,1)} async-done(((bf16[2,1024,768]{2,1,0:T(8,128)(2,1)}), bf16[2,256,768]{2,1,0:T(8,128)(2,1)}) %reduce-scatter.35.cloned.1.call-update) | async-done | bytes 786448 | tf_op jit(solution)/shard_map/reduce_scatter | solution.py:454
  580.7 37.7 %reduce-scatter.33.cloned.1.call-done = bf16[2,256,768]{2,1,0:T(8,128)(2,1)} async-done(((bf16[2,1024,768]{2,1,0:T(8,128)(2,1)}), bf16[2,256,768]{2,1,0:T(8,128)(2,1)}) %reduce-scatter.33.cloned.1.call-update) | async-done | bytes 786448 | tf_op jit(solution)/shard_map/reduce_scatter | solution.py:355
  644.6 7.8 all-gather.45.cloned.1.call-done
  664.3 9.0 convert_reduce_fusion.1
  679.9 10.5 multiply_reduce_fusion
  736.0 7.0 convolution_bitcast_fusion.2
  783.0 68.2 %reduce-scatter.53.cloned.1.call-done = f32[96,576]{1,0:T(8,128)} async-done(((f32[768,576]{1,0:T(8,128)}), f32[96,576]{1,0:T(8,128)}) %reduce-scatter.53.cloned.1.call-update) | async-done | bytes 221200
  854.6 60.2 %reduce-scatter.59.cloned.1.call-done = f32[32,3]{1,0:T(8,128)} async-done(((f32[256,3]{1,0:T(8,128)}), f32[32,3]{1,0:T(8,128)}) %reduce-scatter.59.cloned.1.call-update) | async-done | bytes 400
  916.2 63.4 %reduce-scatter.55.cloned.1.call-done = f32[96,192]{1,0:T(8,128)} async-done(((f32[768,192]{1,0:T(8,128)}), f32[96,192]{1,0:T(8,128)}) %reduce-scatter.55.cloned.1.call-update) | async-done | bytes 73744
  981.4 67.8 %reduce-scatter.51.cloned.1.call-done = f32[96,576]{1,0:T(8,128)} async-done(((f32[768,576]{1,0:T(8,128)}), f32[96,576]{1,0:T(8,128)}) %reduce-scatter.51.cloned.1.call-update) | async-done | bytes 221200
  1053.3 67.1 %reduce-scatter.45.cloned.1.call-done = f32[96,768]{1,0:T(8,128)} async-done(((f32[768,768]{1,0:T(8,128)}), f32[96,768]{1,0:T(8,128)}) %reduce-scatter.45.cloned.1.call-update) | async-done | bytes 294928 | tf_op jit(solution)/shard_map/reduce_scatter | solution.py:494
  1120.4 71.4 %reduce-scatter.43.cloned.1.call-done = f32[96,768]{1,0:T(8,128)} async-done(((f32[768,768]{1,0:T(8,128)}), f32[96,768]{1,0:T(8,128)}) %reduce-scatter.43.cloned.1.call-update) | async-done | bytes 294928 | tf_op jit(solution)/shard_map/reduce_scatter | solution.py:494
  1193.7 69.4 %reduce-scatter.49.cloned.1.call-done = f32[768,96]{0,1:T(8,128)} async-done(((f32[768,768]{0,1:T(8,128)}), f32[768,96]{0,1:T(8,128)}) %reduce-scatter.49.cloned.1.call-update) | async-done | bytes 294928 | tf_op jit(solution)/shard_map/reduce_scatter | solution.py:496
  1263.1 71.3 %reduce-scatter.47.cloned.1.call-done = f32[768,96]{0,1:T(8,128)} async-done(((f32[768,768]{0,1:T(8,128)}), f32[768,96]{0,1:T(8,128)}) %reduce-scatter.47.cloned.1.call-update) | async-done | bytes 294928 | tf_op jit(solution)/shard_map/reduce_scatter | solution.py:496
  1336.3 37.6 %reduce-scatter.41.cloned.1.call-done = bf16[2,256,768]{2,1,0:T(8,128)(2,1)} async-done(((bf16[2,1024,768]{2,1,0:T(8,128)(2,1)}), bf16[2,256,768]{2,1,0:T(8,128)(2,1)}) %reduce-scatter.41.cloned.1.call-update) | async-done | bytes 786448 | tf_op jit(solution)/shard_map/reduce_scatter | solution.py:457
  1374.0 40.5 %reduce-scatter.39.cloned.1.call-done = bf16[2,256,768]{2,1,0:T(8,128)(2,1)} async-done(((bf16[2,1024,768]{2,1,0:T(8,128)(2,1)}), bf16[2,256,768]{2,1,0:T(8,128)(2,1)}) %reduce-scatter.39.cloned.1.call-update) | async-done | bytes 786448 | tf_op jit(solution)/shard_map/reduce_scatter | solution.py:454
  1417.3 37.6 %all-reduce.28 = (f32[768]{0:T(1024)S(1)}, f32[768]{0:T(1024)S(1)}, f32[768]{0:T(1024)S(1)}, f32[768]{0:T(1024)S(1)}, f32[768]{0:T(1024)S(1)}, /*index=5*/f32[76...) all-reduce(f32[768]{0:T(1024)S(1)} %get-tuple-element.207, ...), channel_id=33, replica_groups=mesh['wide'=8,'tensor'=4] {'wide'}, use_global_device_ids=true, to_apply=%region_35.36.clone | all-reduce | flops 8832 | bytes 70656
  (557 shorter events, 319.9 us)
Async XLA Ops:
  7.2 190.2 %all-gather.35.cloned.1.call-start = ((), (), s32[]{:S(2)}) async-start(), calls=%async_computation.16 | async-start | bytes 3932160 | tf_op jit(solution)/shard_map/all_gather | solution.py:323
  61.4 152.2 %all-gather.47.cloned.1.call-start = ((), (), s32[]{:S(2)}) async-start(), calls=%async_computation.32 | async-start | bytes 1327104 | tf_op jit(solution)/shard_map/all_gather | solution.py:221
  62.2 151.4 %all-gather.37.cloned.1.call-start = ((), (), s32[]{:S(2)}) async-start(), calls=%async_computation.17 | async-start | bytes 3932160 | tf_op jit(solution)/shard_map/all_gather | solution.py:324
  62.9 179.9 %all-gather.49.cloned.1.call-start = ((), (), s32[]{:S(2)}) async-start(), calls=%async_computation.33 | async-start | bytes 1327104 | tf_op jit(solution)/shard_map/all_gather | solution.py:223
  63.8 223.8 %reduce-scatter.31.cloned.1.call-start = ((), (), s32[]{:S(2)}) async-start(), calls=%async_computation.18 | async-start | bytes 3932160 | tf_op jit(solution)/shard_map/reduce_scatter | solution.py:355
  95.8 434.9 %copy-start.55 = (f32[1024,8]{0,1:T(8,128)}, f32[1024,8]{0,1:T(8,128)S(1)}, u32[]{:S(2)}) copy-start(f32[1024,8]{0,1:T(8,128)S(1)} %get-tuple-element.311) | copy-start | bytes 98308
  250.7 174.8 %all-gather.43.cloned.1.call-start = ((), (), s32[]{:S(2)}) async-start(), calls=%async_computation.22 | async-start | bytes 3932160 | tf_op jit(solution)/shard_map/all_gather | solution.py:407
  251.3 178.5 %all-gather.51.cloned.1.call-start = ((), (), s32[]{:S(2)}) async-start(), calls=%async_computation.34 | async-start | bytes 1327104 | tf_op jit(solution)/shard_map/all_gather | solution.py:221
  252.1 177.8 %all-gather.41.cloned.1.call-start = ((), (), s32[]{:S(2)}) async-start(), calls=%async_computation.20 | async-start | bytes 3932160 | tf_op jit(solution)/shard_map/all_gather | solution.py:324
  292.7 162.3 %all-gather.39.cloned.1.call-start = ((), (), s32[]{:S(2)}) async-start(), calls=%async_computation.19 | async-start | bytes 3932160 | tf_op jit(solution)/shard_map/all_gather | solution.py:323
  293.4 178.8 %all-gather.53.cloned.1.call-start = ((), (), s32[]{:S(2)}) async-start(), calls=%async_computation.35 | async-start | bytes 1327104 | tf_op jit(solution)/shard_map/all_gather | solution.py:223
  294.0 265.2 %reduce-scatter.37.cloned.1.call-start = ((), (), s32[]{:S(2)}) async-start(), calls=%async_computation.24 | async-start | bytes 3932160 | tf_op jit(solution)/shard_map/reduce_scatter | solution.py:457
  489.0 88.7 %reduce-scatter.35.cloned.1.call-start = ((), (), s32[]{:S(2)}) async-start(), calls=%async_computation.23 | async-start | bytes 3932160 | tf_op jit(solution)/shard_map/reduce_scatter | solution.py:454
  540.7 77.7 %reduce-scatter.33.cloned.1.call-start = ((), (), s32[]{:S(2)}) async-start(), calls=%async_computation.21 | async-start | bytes 3932160 | tf_op jit(solution)/shard_map/reduce_scatter | solution.py:355
  558.6 93.8 %all-gather.45.cloned.1.call-start = ((), (), s32[]{:S(2)}) async-start(), calls=%async_computation.25 | async-start | bytes 3932160 | tf_op jit(solution)/shard_map/all_gather | solution.py:407
  623.7 157.5 %reduce-scatter.61.cloned.1.call-start = ((), (), s32[]{:S(2)}) async-start(), calls=%async_computation.41 | async-start | bytes 147456
  624.7 157.4 %reduce-scatter.57.cloned.1.call-start = ((), (), s32[]{:S(2)}) async-start(), calls=%async_computation.39 | async-start | bytes 884736
  628.9 222.4 %reduce-scatter.53.cloned.1.call-start = ((), (), s32[]{:S(2)}) async-start(), calls=%async_computation.37 | async-start | bytes 2211840
  644.6 270.3 %reduce-scatter.59.cloned.1.call-start = ((), (), s32[]{:S(2)}) async-start(), calls=%async_computation.40 | async-start | bytes 147456
  702.9 276.8 %reduce-scatter.55.cloned.1.call-start = ((), (), s32[]{:S(2)}) async-start(), calls=%async_computation.38 | async-start | bytes 884736
  713.6 335.6 %reduce-scatter.51.cloned.1.call-start = ((), (), s32[]{:S(2)}) async-start(), calls=%async_computation.36 | async-start | bytes 2211840
  736.0 384.4 %reduce-scatter.45.cloned.1.call-start = ((), (), s32[]{:S(2)}) async-start(), calls=%async_computation.29 | async-start | bytes 2654208 | tf_op jit(solution)/shard_map/reduce_scatter | solution.py:494
  743.0 448.8 %reduce-scatter.43.cloned.1.call-start = ((), (), s32[]{:S(2)}) async-start(), calls=%async_computation.28 | async-start | bytes 2654208 | tf_op jit(solution)/shard_map/reduce_scatter | solution.py:494
  750.0 513.1 %reduce-scatter.49.cloned.1.call-start = ((), (), s32[]{:S(2)}) async-start(), calls=%async_computation.31 | async-start | bytes 2654208 | tf_op jit(solution)/shard_map/reduce_scatter | solution.py:496
  757.0 577.4 %reduce-scatter.47.cloned.1.call-start = ((), (), s32[]{:S(2)}) async-start(), calls=%async_computation.30 | async-start | bytes 2654208 | tf_op jit(solution)/shard_map/reduce_scatter | solution.py:496
  764.3 609.7 %reduce-scatter.41.cloned.1.call-start = ((), (), s32[]{:S(2)}) async-start(), calls=%async_computation.27 | async-start | bytes 3932160 | tf_op jit(solution)/shard_map/reduce_scatter | solution.py:457
  770.8 643.7 %reduce-scatter.39.cloned.1.call-start = ((), (), s32[]{:S(2)}) async-start(), calls=%async_computation.26 | async-start | bytes 3932160 | tf_op jit(solution)/shard_map/reduce_scatter | solution.py:454
  980.6 433.9 %copy-start.90 = (f32[768]{0:T(1024)S(1)}, f32[768]{0:T(1024)}, u32[]{:S(2)}) copy-start(f32[768]{0:T(1024)} %copy-done.89) | copy-start | bytes 9220
  980.6 433.9 %copy-start.92 = (f32[768]{0:T(1024)S(1)}, f32[768]{0:T(1024)}, u32[]{:S(2)}) copy-start(f32[768]{0:T(1024)} %copy-done.91) | copy-start | bytes 9220
  980.6 433.9 %copy-start.94 = (f32[2,256]{1,0:T(2,128)S(1)}, f32[2,256]{1,0:T(2,128)}, u32[]{:S(2)}) copy-start(f32[2,256]{1,0:T(2,128)} %copy-done.93) | copy-start | bytes 6148
  980.7 433.9 %copy-start.98 = (f32[2,256]{1,0:T(2,128)S(1)}, f32[2,256]{1,0:T(2,128)}, u32[]{:S(2)}) copy-start(f32[2,256]{1,0:T(2,128)} %copy-done.97) | copy-start | bytes 6148
  1052.2 365.1 %copy-start.106 = (f32[768]{0:T(1024)S(1)}, f32[768]{0:T(1024)}, u32[]{:S(2)}) copy-start(f32[768]{0:T(1024)} %get-tuple-element.257) | copy-start | bytes 9220
  (125 other events, 3085.4 us)
Sparse Core Ops, SparseCore 0:
  61.5 25.8 all-gather.34
  89.5 43.6 all-gather.46
  135.3 28.5 all-gather.36
  166.0 41.8 all-gather.48
  250.9 36.6 reduce-scatter.30
  289.1 28.5 all-gather.42
  320.6 44.9 all-gather.50
  367.8 27.2 all-gather.40
  397.4 28.5 all-gather.38
  428.2 41.0 all-gather.52
  489.1 37.0 reduce-scatter.36
  540.8 36.8 reduce-scatter.34
  580.4 37.9 reduce-scatter.32
  623.8 28.5 all-gather.44
  656.1 60.8 reduce-scatter.60
  720.1 61.5 reduce-scatter.56
  785.4 65.7 reduce-scatter.52
  855.0 59.8 reduce-scatter.58
  918.2 61.4 reduce-scatter.54
  983.4 65.7 reduce-scatter.50
  1052.7 67.6 reduce-scatter.44
  1123.9 67.8 reduce-scatter.42
  1195.3 67.7 reduce-scatter.48
  1266.5 67.9 reduce-scatter.46
  1337.0 36.9 reduce-scatter.40
  1376.5 37.9 reduce-scatter.38
where the time goes:
time: 1480 us
  waiting for transfers between devices  720 us (49%)
  blocking collectives  341 us (23%)
  matrix products  218 us (15%)
  other arithmetic  112 us (8%)
  local copies, waits for them, and re-layouts  63.7 us (4%)
  between operations  18.7 us (1%)
    unnamed x32, waiting for transfers between devices  263 us
    reduce_scatter x2, waiting for transfers between devices, body(): lax.psum_scatter(members[10], 'wide', scatter_dimension=1, tiled=True)  141 us
    reduce_scatter x2, waiting for transfers between devices, body(): lax.psum_scatter(members[8], 'wide', scatter_dimension=0, tiled=True)  138 us
    unnamed x2, blocking collectives  77 us
    reduce_scatter x2, waiting for transfers between devices, body(): lax.psum_scatter(partial_sum.astype(jnp.bfloat16), 'tensor', scatter_dime...  73 us
    all_gather x2, blocking collectives, fetch_layer(): lax.all_gather(query_key_value_weight[layer_idx], 'wide', axis=1, tiled=T...  69.6 us
    all_gather x2, blocking collectives, fetch_layer(): lax.all_gather(output_weight[layer_idx], 'wide', axis=1, tiled=True)  65.4 us
    all_gather x2, blocking collectives, fetch_layer(): lax.all_gather(up_bias[layer_idx], 'wide', axis=1, tiled=True)  61.9 us
  transfers between devices with their start and end apart: 26, of which 14 were waited for; matrix products, arithmetic and copies ran while one was open for 22% of the time, Pallas kernels for 0%

commit v1 on v0

v1 whole, which is shorter than its diff:
```python
import math

import jax
import jax.numpy as jnp
from jax import lax
from jax.experimental import pallas as pl
from jax.experimental.pallas import tpu as pltpu
from jax.sharding import PartitionSpec as P

HD = 64
ROT = 16
EPSILON = 1e-05
Q_ROWS = 256
BF = jnp.bfloat16
F32 = jnp.float32

NN = (((1,), (0,)), ((), ()))
NT = (((1,), (1,)), ((), ()))
TN = (((0,), (0,)), ((), ()))


def dot(a, b, dims):
    return lax.dot_general(a, b, dims, preferred_element_type=F32)


def rotary_planes(seq_len, heads):
    half = ROT // 2
    positions = jnp.arange(seq_len, dtype=F32)
    inverse = jnp.exp(jnp.arange(half, dtype=F32) * (-2.0 * math.log(10000.0) / ROT))
    angles = positions[:, None] * inverse[None, :]
    cos, sin = jnp.cos(angles), jnp.sin(angles)
    zero = jnp.zeros((seq_len, half), F32)
    rest0 = jnp.zeros((seq_len, HD - ROT), F32)
    same = jnp.concatenate([cos, cos, rest0 + 1.0], axis=1)
    ahead = jnp.concatenate([-sin, zero, rest0], axis=1)
    behind = jnp.concatenate([zero, sin, rest0], axis=1)

    def spread(plane, fill):
        return jnp.concatenate(
            [jnp.tile(plane, (1, 2 * heads)), jnp.full((seq_len, heads * HD), fill, F32)], axis=1
        )

    return spread(same, 1.0), spread(ahead, 0.0), spread(behind, 0.0)


def rotate(u, planes, sign):
    same, ahead, behind = planes
    half = ROT // 2
    return u * same + sign * (
        jnp.roll(u, -half, axis=1) * ahead + jnp.roll(u, half, axis=1) * behind
    )


def transposed_probs(q, k, row0, end):
    rows = q.shape[0]
    scores = dot(k, q, NT) * (1.0 / math.sqrt(HD))
    key_pos = lax.broadcasted_iota(jnp.int32, (end, rows), 0)
    query_pos = row0 + lax.broadcasted_iota(jnp.int32, (end, rows), 1)
    scores = jnp.where(key_pos <= query_pos, scores, -1e30)
    exps = jnp.exp(scores - jnp.max(scores, axis=0, keepdims=True))
    return exps * (1.0 / jnp.sum(exps, axis=0, keepdims=True))


def attend_kernel(heads, qkv_ref, out_ref):
    seq_len = qkv_ref.shape[0]
    width = heads * HD
    for h in range(heads):
        lanes = slice(h * HD, (h + 1) * HD)
        for row0 in range(0, seq_len, Q_ROWS):
            end = row0 + Q_ROWS
            q = qkv_ref[row0:end, h * HD:(h + 1) * HD]
            k = qkv_ref[0:end, width + h * HD:width + (h + 1) * HD]
            v = qkv_ref[0:end, 2 * width + h * HD:2 * width + (h + 1) * HD]
            probs = transposed_probs(q, k, row0, end).astype(BF)
            out_ref[row0:end, lanes] = dot(v, probs, TN).T.astype(BF)


def attend_back_kernel(heads, qkv_ref, grad_ref, out_ref):
    seq_len = qkv_ref.shape[0]
    width = heads * HD
    scale = 1.0 / math.sqrt(HD)
    for h in range(heads):
        lq = slice(h * HD, (h + 1) * HD)
        lk = slice(width + h * HD, width + (h + 1) * HD)
        lv = slice(2 * width + h * HD, 2 * width + (h + 1) * HD)
        for row0 in reversed(range(0, seq_len, Q_ROWS)):
            end = row0 + Q_ROWS
            q = qkv_ref[row0:end, lq]
            k = qkv_ref[0:end, lk]
            v = qkv_ref[0:end, lv]
            d_out = grad_ref[row0:end, lq]
            probs = transposed_probs(q, k, row0, end)
            d_probs = dot(v, d_out, NT)
            delta = jnp.sum(probs * d_probs, axis=0, keepdims=True)
            d_scores = (probs * (d_probs - delta)).astype(BF)
            out_ref[row0:end, lq] = dot(k, d_scores, TN).T * scale
            d_k = dot(d_scores, q, NN) * scale
            d_v = dot(probs.astype(BF), d_out, NN)
            if end == seq_len:
                out_ref[:, lk] = d_k
                out_ref[:, lv] = d_v
            else:
                out_ref[0:end, lk] = out_ref[0:end, lk] + d_k
                out_ref[0:end, lv] = out_ref[0:end, lv] + d_v


def whole_blocks(count):
    return [pl.BlockSpec(memory_space=pltpu.VMEM)] * count


def attend(qkv, heads):
    seq_len = qkv.shape[0]

    def run(qkv_ref, out_ref):
        attend_kernel(heads, qkv_ref, out_ref)

    return pl.pallas_call(
        run,
        out_shape=jax.ShapeDtypeStruct((seq_len, heads * HD), BF),
        in_specs=whole_blocks(1),
        out_specs=whole_blocks(1)[0],
        compiler_params=pltpu.CompilerParams(vmem_limit_bytes=32 * 2**20),
        cost_estimate=pl.CostEstimate(
            flops=4 * heads * seq_len * seq_len * HD,
            bytes_accessed=8 * seq_len * heads * HD,
            transcendentals=heads * seq_len * seq_len // 2,
        ),
    )(qkv)


def attend_back(qkv, grad_heads, heads):
    seq_len = qkv.shape[0]

    def run(qkv_ref, grad_ref, out_ref):
        attend_back_kernel(heads, qkv_ref, grad_ref, out_ref)

    return pl.pallas_call(
        run,
        out_shape=jax.ShapeDtypeStruct((seq_len, 3 * heads * HD), F32),
        in_specs=whole_blocks(2),
        out_specs=whole_blocks(1)[0],
        compiler_params=pltpu.CompilerParams(vmem_limit_bytes=32 * 2**20),
        cost_estimate=pl.CostEstimate(
            flops=10 * heads * seq_len * seq_len * HD,
            bytes_accessed=20 * seq_len * heads * HD,
            transcendentals=heads * seq_len * seq_len // 2,
        ),
    )(qkv, grad_heads)


def normalize_rows(residual):
    mean_val = jnp.mean(residual, axis=-1, keepdims=True)
    centered = residual - mean_val
    variance = jnp.mean(centered * centered, axis=-1, keepdims=True)
    inv_std = lax.rsqrt(variance + EPSILON)
    return centered * inv_std, inv_std


def swap(x, bit, size):
    return lax.ppermute(x, "tensor", [(i, i ^ bit) for i in range(size)])


def gather_rows(x, size):
    me = lax.axis_index("tensor")
    far = swap(x, 2, size)
    parts = [x, swap(x, 1, size), far, swap(far, 1, size)]
    rows = x.shape[0]
    full = jnp.zeros((size * rows,) + x.shape[1:], x.dtype)
    for k, part in enumerate(parts):
        full = lax.dynamic_update_slice(full, part, ((me ^ k) * rows, 0))
    return full


def scatter_rows(partial, size):
    me = lax.axis_index("tensor")
    core, chip = me % 2, me // 2
    rows = partial.shape[0] // size
    pieces = partial.reshape(2, 2, rows, partial.shape[1])
    away = lax.dynamic_index_in_dim(pieces, 1 - core, 1, keepdims=False)
    kept = lax.dynamic_index_in_dim(pieces, core, 1, keepdims=False)
    both = kept.astype(F32) + swap(away, 1, size).astype(F32)
    off = lax.dynamic_index_in_dim(both, 1 - chip, 0, keepdims=False).astype(BF)
    mine = lax.dynamic_index_in_dim(both, chip, 0, keepdims=False)
    return mine + swap(off, 2, size).astype(F32)


def gather_weights(x):
    return lax.all_gather(x, "wide", axis=0, tiled=True)


def sum_to_owner(x, size):
    rows = x.shape[0] // size
    pieces = x.astype(BF).reshape(size, rows, x.shape[1])
    return jnp.sum(
        lax.all_to_all(pieces, "wide", 0, 0).astype(F32), axis=0
    )


def body(
    tokens,
    cotangent,
    ln1_gain,
    ln1_bias,
    ln2_gain,
    ln2_bias,
    qkv_weight,
    qkv_bias,
    dense_weight,
    dense_bias,
    fc1_weight,
    fc1_bias,
    fc2_weight,
    fc2_bias,
):
    wide = lax.axis_size("wide")
    tensor = lax.axis_size("tensor")
    w_me = lax.axis_index("wide")
    layers = qkv_weight.shape[0]
    seqs = tokens.shape[0]
    local_len, model = tokens.shape[1:]
    seq_len = local_len * tensor
    own = ln1_gain.shape[1]
    heads = qkv_bias.shape[2]
    groups = fc1_bias.shape[1]
    att = heads * HD
    hid = fc1_weight.shape[2]
    planes = rotary_planes(seq_len, heads)

    first_own, w1, w2, offset_parts = [], [], [], []
    for l in range(layers):
        qkv_own = jnp.concatenate([qkv_weight[l, c] for c in range(3)], axis=1)
        up_own = fc1_weight[l]
        first_own.append((up_own.astype(F32), qkv_own.astype(F32)))
        folded = jnp.concatenate(
            [
                up_own.astype(F32) * ln2_gain[l].astype(F32)[:, None],
                qkv_own.astype(F32) * ln1_gain[l].astype(F32)[:, None],
            ],
            axis=1,
        ).astype(BF)
        w1.append(gather_weights(folded))
        w2.append(
            gather_weights(jnp.concatenate([fc2_weight[l].T, dense_weight[l].T], axis=1))
        )
        up_b = jnp.zeros((groups, hid // groups), F32)
        up_b = lax.dynamic_update_slice(
            up_b, fc1_bias[l].astype(F32), (0, w_me * fc1_bias.shape[2])
        )
        qkv_b = jnp.zeros((3, heads, HD), F32)
        qkv_b = lax.dynamic_update_slice(
            qkv_b, qkv_bias[l].astype(F32), (0, 0, w_me * qkv_bias.shape[3])
        )
        out_b = jnp.zeros((model,), F32)
        out_b = lax.dynamic_update_slice(
            out_b, dense_bias[l].astype(F32) + fc2_bias[l].astype(F32), (w_me * own,)
        )
        shift_b = jnp.sum(ln2_bias[l].astype(F32)[:, None] * up_own.astype(F32), axis=0)
        shift_a = jnp.sum(ln1_bias[l].astype(F32)[:, None] * qkv_own.astype(F32), axis=0)
        offset_parts.append(
            jnp.concatenate([shift_b + up_b.reshape(-1), shift_a + qkv_b.reshape(-1), out_b])
        )
    offsets = lax.psum(jnp.stack(offset_parts), "wide")

    residual = [tokens[s].astype(F32) for s in range(seqs)]
    saved = []
    for l in range(layers):
        up_off = offsets[l, :hid]
        qkv_off = offsets[l, hid:hid + 3 * att]
        out_off = offsets[l, hid + 3 * att:]
        per_seq = []
        for s in range(seqs):
            scaled, inv_std = normalize_rows(residual[s])
            if l == 0:
                full_tokens = gather_rows(tokens[s], tensor)
                full = normalize_rows(full_tokens.astype(F32))[0].astype(BF)
            else:
                full = gather_rows(scaled.astype(BF), tensor)
            lin = dot(full, w1[l][:, hid:], NN) + qkv_off
            qkv = rotate(lin, planes, 1.0).astype(BF)
            heads_out = attend(qkv, heads)
            hidden = dot(full, w1[l][:, :hid], NN) + up_off
            phi = 0.5 + 0.5 * lax.erf(hidden * math.sqrt(0.5))
            act = (hidden * phi).astype(BF)
            slope = (
                phi + hidden * jnp.exp(-0.5 * hidden * hidden) * (1.0 / math.sqrt(2.0 * math.pi))
            ).astype(BF)
            partial = dot(act, w2[l][:, :hid], NT) + dot(heads_out, w2[l][:, hid:], NT)
            branch = scatter_rows(partial.astype(BF), tensor)
            residual[s] = residual[s] + branch + out_off
            per_seq.append((scaled, inv_std, full, qkv, heads_out, act, slope))
        saved.append(per_seq)
    mixed = jnp.stack([r.astype(BF) for r in residual])

    grad = [cotangent[s].astype(F32) for s in range(seqs)]
    outs = [None] * layers
    for l in reversed(range(layers)):
        bias_part = sum(jnp.sum(g, axis=0) for g in grad)
        w_up, w_qkv = w1[l][:, :hid], w1[l][:, hid:]
        w_down, w_out = w2[l][:, :hid], w2[l][:, hid:]
        full_grad, d_hid, d_lin = [], [], []
        for s in range(seqs):
            scaled, inv_std, full, qkv, heads_out, act, slope = saved[l][s]
            g_full = gather_rows(grad[s].astype(BF), tensor)
            d_heads = dot(g_full, w_out, NN).astype(BF)
            d_hidden = (dot(g_full, w_down, NN) * slope.astype(F32)).astype(BF)
            d_qkv = rotate(attend_back(qkv, d_heads, heads), planes, -1.0).astype(BF)
            e_part = dot(d_hidden, w_up, NT) + dot(d_qkv, w_qkv, NT)
            e = scatter_rows(e_part.astype(BF), tensor)
            mean_e = jnp.mean(e, axis=-1, keepdims=True)
            mean_x = jnp.mean(e * scaled, axis=-1, keepdims=True)
            grad[s] = grad[s] + inv_std * (e - mean_e - scaled * mean_x)
            full_grad.append(g_full)
            d_hid.append(d_hidden)
            d_lin.append(d_qkv)
        grads_of = lambda lefts, rights: sum(dot(a, b, TN) for a, b in zip(lefts, rights))
        fulls = [saved[l][s][2] for s in range(seqs)]
        down_grad = sum_to_owner(grads_of(full_grad, [saved[l][s][5] for s in range(seqs)]), wide)
        out_grad = sum_to_owner(grads_of(full_grad, [saved[l][s][4] for s in range(seqs)]), wide)
        up_raw = sum_to_owner(grads_of(fulls, d_hid), wide)
        qkv_raw = sum_to_owner(grads_of(fulls, d_lin), wide)
        up_db = sum(jnp.sum(d.astype(F32), axis=0) for d in d_hid)
        qkv_db = sum(jnp.sum(d.astype(F32), axis=0) for d in d_lin)
        outs[l] = (down_grad, out_grad, up_raw, qkv_raw, up_db, qkv_db, bias_part)
    input_grad = jnp.stack([g.astype(BF) for g in grad])

    db_all = lax.psum(
        jnp.stack([jnp.concatenate([outs[l][4], outs[l][5]]) for l in range(layers)]), "wide"
    )
    bias_all = lax.psum(jnp.stack([outs[l][6] for l in range(layers)]), ("wide", "tensor"))
    out_bias_grad = lax.dynamic_slice(bias_all, (0, w_me * own), (layers, own))
    norm_parts, weight_grads = [], []
    for l in range(layers):
        down_grad, out_grad, up_raw, qkv_raw = outs[l][:4]
        up_db, qkv_db = db_all[l, :hid], db_all[l, hid:]
        up_own, qkv_own = first_own[l]
        norm_parts.append(
            jnp.stack(
                [
                    jnp.sum(qkv_raw * qkv_own, axis=1),
                    jnp.sum(qkv_own * qkv_db[None, :], axis=1),
                    jnp.sum(up_raw * up_own, axis=1),
                    jnp.sum(up_own * up_db[None, :], axis=1),
                ]
            )
        )
        col = lambda v: v[l].astype(F32)[:, None]
        up_grad = col(ln2_gain) * up_raw + col(ln2_bias) * up_db[None, :]
        qkv_grad = col(ln1_gain) * qkv_raw + col(ln1_bias) * qkv_db[None, :]
        qkv_grad = jnp.stack([qkv_grad[:, c * att:(c + 1) * att] for c in range(3)])
        qkv_bg = lax.dynamic_slice(
            qkv_db.reshape(3, heads, HD), (0, 0, w_me * qkv_bias.shape[3]),
            (3, heads, qkv_bias.shape[3]),
        )
        up_bg = lax.dynamic_slice(
            up_db.reshape(groups, -1), (0, w_me * fc1_bias.shape[2]), (groups, fc1_bias.shape[2])
        )
        weight_grads.append((qkv_grad, qkv_bg, out_grad.T, up_grad, up_bg, down_grad.T))
    norms = lax.psum(jnp.stack(norm_parts), "tensor")
    wg = [jnp.stack([weight_grads[l][m] for l in range(layers)]) for m in range(6)]
    return (
        mixed,
        input_grad,
        norms[:, 0],
        norms[:, 1],
        norms[:, 2],
        norms[:, 3],
        wg[0],
        wg[1],
        wg[2],
        out_bias_grad,
        wg[3],
        wg[4],
        wg[5],
        out_bias_grad,
    )


def solution(mesh):
    specs = (
        P("wide", "tensor", None),
        P("wide", "tensor", None),
        P(None, "wide"),
        P(None, "wide"),
        P(None, "wide"),
        P(None, "wide"),
        P(None, None, "wide", "tensor"),
        P(None, None, "tensor", "wide"),
        P(None, "tensor", "wide"),
        P(None, "wide"),
        P(None, "wide", "tensor"),
        P(None, "tensor", "wide"),
        P(None, "tensor", "wide"),
        P(None, "wide"),
    )
    return jax.shard_map(body, mesh=mesh, in_specs=specs, out_specs=specs, check_vma=False)
```

time: 1480 us -> 719 us (0.49)
  waiting for transfers between devices: 720 us -> 162 us
  blocking collectives: 341 us -> 128 us
  matrix products: 218 us -> 128 us
  Pallas kernels: 0 us -> 65.7 us
  starting transfers between devices: 1.72 us -> 58.5 us
  other arithmetic: 112 us -> 63.1 us
  local copies, waits for them, and re-layouts: 63.7 us -> 90.5 us
    reduce_scatter x10 -> x0, waiting for transfers between devices: 449 us -> none  [the longest x2 141 us: body(): lax.psum_scatter(members[10], 'wide', scatter_dimension=1, tiled=True)]
    unnamed x32 -> x4, waiting for transfers between devices: 263 us -> 0.07 us
    all_gather x8 -> x0, blocking collectives: 258 us -> none  [the longest x2 69.6 us: fetch_layer(): lax.all_gather(query_key_value_weight[layer_idx], 'wide', axis=1, tiled=T...]
    psum x1 -> x4, blocking collectives: 6.01 us -> 128 us  [the longest x1 43.7 us: body(): lax.psum(jnp.stack([outs[l][6] for l in range(layers)]), ('wide', 'tensor'))]
    dot_general x48, matrix products: 218 us -> 128 us  [dot(): return lax.dot_general(a, b, dims, preferred_element_type=F32)]
    unnamed x2 -> x0, blocking collectives: 77 us -> none
    pallas_call x0 -> x8, Pallas kernels: none -> 65.7 us  [the longest x4 40 us: attend_back(): pl.pallas_call(run, out_shape=jax.ShapeDtypeStruct((seq_len, 3 * heads *...]
    all_to_all x0 -> x8, waiting for transfers between devices: none -> 57.5 us  [sum_to_owner(): return jnp.sum(lax.all_to_all(pieces, 'wide', 0, 0).astype(F32), axis=0)]
  transfers between devices with their start and end apart: 26 -> 52, of which waited for: 14 -> 15; matrix products, arithmetic and copies ran while one was open for 22% -> 32% of each run, Pallas kernels for 0% -> 5%
where the time goes in v1:
time: 719 us; the launch traced here: 713 us
  waiting for transfers between devices  162 us (23%)
  blocking collectives  128 us (18%)
  matrix products  128 us (18%)
  local copies, waits for them, and re-layouts  90.5 us (13%)
  Pallas kernels  65.7 us (9%)
  other arithmetic  63.1 us (9%)
  starting transfers between devices  58.5 us (8%)
  between operations  17.5 us (2%)
    dot_general x48, matrix products, dot(): return lax.dot_general(a, b, dims, preferred_element_type=F32)  128 us
    all_gather x4, waiting for transfers between devices, gather_weights(): return lax.all_gather(x, 'wide', axis=0, tiled=True)  58.3 us
    all_to_all x8, waiting for transfers between devices, sum_to_owner(): return jnp.sum(lax.all_to_all(pieces, 'wide', 0, 0).astype(F32), axis=0)  57.5 us
    ppermute x40, waiting for transfers between devices, swap(): return lax.ppermute(x, 'tensor', [(i, i ^ bit) for i in range(size)])  46 us
    psum x1, blocking collectives, body(): lax.psum(jnp.stack([outs[l][6] for l in range(layers)]), ('wide', 'tensor'))  43.7 us
    pallas_call x4, Pallas kernels, attend_back(): pl.pallas_call(run, out_shape=jax.ShapeDtypeStruct((seq_len, 3 * heads *...  40 us
    psum x1, blocking collectives, body(): offsets = lax.psum(jnp.stack(offset_parts), 'wide')  39.2 us
    psum x1, blocking collectives, body(): lax.psum(jnp.stack([jnp.concatenate([outs[l][4], outs[l][5]]) for l in ra...  37.5 us
  transfers between devices with their start and end apart: 52, of which 15 were waited for; matrix products, arithmetic and copies ran while one was open for 32% of the time, Pallas kernels for 5%

profile of v1, /device:TPU:0, one launch (start us, length us, event | category | flops | bytes accessed | tf_op | source)
XLA Modules:
  0.0 713.0 jit_solution(5455359858695689719)
XLA Ops:
  27.8 39.2 %psum.28 = f32[2,2112]{1,0:T(2,128)S(1)} all-reduce(f32[2,2112]{1,0:T(2,128)S(1)} %pad_maximum_fusion.12), channel_id=1, replica_groups=mesh['wide'=8,'tensor'=4] {'wide'}, use_global_device_ids=true, to_apply=%region_6.0 | all-reduce | flops 4224 | bytes 33792 | tf_op jit(solution)/shard_map/psum | solution.py:262
  98.4 6.6 shard_map.245
  109.8 4.8 multiply_convert_fusion.7
  130.9 4.9 collective-permute-done.4
  140.8 16.1 %all-gather.11.cloned.1.call-done = bf16[768,960]{1,0:T(8,128)(2,1)} async-done(((bf16[96,960]{1,0:T(8,128)(2,1)}), bf16[768,960]{1,0:T(8,128)(2,1)}) %all-gather.11.cloned.1.call-update) | async-done | bytes 1474576 | tf_op jit(solution)/shard_map/all_gather | solution.py:188
  165.6 42.2 %all-gather.9.cloned.1.call-done = bf16[768,1344]{1,0:T(8,128)(2,1)} async-done(((bf16[96,1344]{1,0:T(8,128)(2,1)}), bf16[768,1344]{1,0:T(8,128)(2,1)}) %all-gather.9.cloned.1.call-update) | async-done | bytes 2064400 | tf_op jit(solution)/shard_map/all_gather | solution.py:188
  214.5 6.4 shard_map.246
  220.9 10.0 %shard_map.249 = f32[1024,576]{1,0:T(8,128)S(1)} custom-call(bf16[1024,576]{1,0:T(8,128)(2,1)S(1)} %fusion.31.qkv_ref, bf16[1024,192]{1,0:T(8,128)(2,1)S(1)} %copy.113.grad_ref), custom_call_target="tpu_custom_call" | custom-call | flops 2013265920 | bytes 3932160 | tf_op jit(solution)/shard_map/pallas_call | solution.py:137
  253.0 9.6 %collective-permute-done.24 = bf16[256,768]{1,0:T(8,128)(2,1)S(1)} collective-permute-done((bf16[256,768]{1,0:T(8,128)(2,1)S(1)}, bf16[256,768]{1,0:T(8,128)(2,1)S(1)}, u32[]{:S(2)}, u32[]{:S(2)}) %collective-permute-start.24) | collective-permute-done | bytes 393248 | tf_op jit(solution)/shard_map/ppermute | solution.py:160
  263.0 7.2 %collective-permute-done.9 = bf16[256,768]{1,0:T(8,128)(2,1)S(1)} collective-permute-done((bf16[256,768]{1,0:T(8,128)(2,1)S(1)}, bf16[256,768]{1,0:T(8,128)(2,1)S(1)}, u32[]{:S(2)}, u32[]{:S(2)}) %collective-permute-start.9) | collective-permute-done | bytes 393248 | tf_op jit(solution)/shard_map/ppermute | solution.py:160
  288.6 10.1 %shard_map.250 = f32[1024,576]{1,0:T(8,128)S(1)} custom-call(bf16[1024,576]{1,0:T(8,128)(2,1)S(1)} %fusion.29.qkv_ref, bf16[1024,192]{1,0:T(8,128)(2,1)S(1)} %copy.115.grad_ref), custom_call_target="tpu_custom_call" | custom-call | flops 2013265920 | bytes 3932160 | tf_op jit(solution)/shard_map/pallas_call | solution.py:137
  307.0 6.2 shard_map.247
  325.6 8.0 %collective-permute-done.14 = bf16[256,768]{1,0:T(8,128)(2,1)S(1)} collective-permute-done((bf16[256,768]{1,0:T(8,128)(2,1)S(1)}, bf16[256,768]{1,0:T(8,128)(2,1)S(1)}, u32[]{:S(2)}, u32[]{:S(2)}) %collective-permute-start.14) | collective-permute-done | bytes 393248 | tf_op jit(solution)/shard_map/ppermute | solution.py:160
  338.0 7.1 collective-permute-done.16
  353.2 6.4 shard_map.248
  359.6 10.0 %shard_map.251 = f32[1024,576]{1,0:T(8,128)S(1)} custom-call(bf16[1024,576]{1,0:T(8,128)(2,1)S(1)} %fusion.35.qkv_ref, bf16[1024,192]{1,0:T(8,128)(2,1)S(1)} %copy.117.grad_ref), custom_call_target="tpu_custom_call" | custom-call | flops 2013265920 | bytes 3932160 | tf_op jit(solution)/shard_map/pallas_call | solution.py:137
  404.8 4.4 add_convert_fusion.12
  426.3 6.0 all-to-all-start.2
  433.9 6.0 collective-permute-done.19
  445.4 43.7 %psum.31 = f32[2,768]{1,0:T(2,128)S(1)} all-reduce(f32[2,768]{1,0:T(2,128)S(1)} %pad_maximum_fusion.17), channel_id=1, replica_groups=mesh['wide'=8,'tensor'=4] {'wide','tensor'}, use_global_device_ids=true, to_apply=%region_53.54 | all-reduce | flops 1536 | bytes 12288 | tf_op jit(solution)/shard_map/psum | solution.py:329
  490.7 4.7 all-to-all-start.7
  502.6 9.9 %shard_map.252 = f32[1024,576]{1,0:T(8,128)S(1)} custom-call(bf16[1024,576]{1,0:T(8,128)(2,1)S(1)} %get-tuple-element.127.qkv_ref, bf16[1024,192]{1,0:T(8,128)(2,1)S(1)} %copy.119.grad_ref), custom_call_target="tpu_custom_call" | custom-call | flops 2013265920 | bytes 3932160 | tf_op jit(solution)/shard_map/pallas_call | solution.py:137
  515.1 5.5 convert_reduce_fusion.4
  523.0 37.5 %psum.29 = f32[2,1344]{1,0:T(2,128)S(1)} all-reduce(f32[2,1344]{1,0:T(2,128)S(1)} %pad_maximum_fusion.14), channel_id=1, replica_groups=mesh['wide'=8,'tensor'=4] {'wide'}, use_global_device_ids=true, to_apply=%region_35.36 | all-reduce | flops 2688 | bytes 21504 | tf_op jit(solution)/shard_map/psum | solution.py:326
  566.2 4.3 fusion.179
  588.3 4.5 fusion.177
  601.2 5.3 add_convert_fusion.11
  606.5 4.7 all-to-all-done.4
  628.0 11.1 %all-to-all-done = bf16[8,96,576]{2,1,0:T(8,128)(2,1)} async-done(((bf16[8,96,576]{2,1,0:T(8,128)(2,1)}), bf16[8,96,576]{2,1,0:T(8,128)(2,1)}, u32[]{:S(2)}, u32[]{:S(2)}) %all-to-all-start) | async-done | bytes 884768 | tf_op jit(solution)/shard_map/all_to_all | solution.py:195
  650.4 20.9 %all-to-all-done.1 = bf16[8,96,768]{2,1,0:T(8,128)(2,1)S(1)} async-done(((bf16[8,96,768]{2,1,0:T(8,128)(2,1)}), bf16[8,96,768]{2,1,0:T(8,128)(2,1)S(1)}, u32[]{:S(2)}, u32[]{:S(2)}) %all-to-all-start.1) | async-done | bytes 1179680 | tf_op jit(solution)/shard_map/all_to_all | solution.py:195
  679.0 7.0 psum.30
  686.8 16.9 %all-to-all-done.6 = bf16[8,96,768]{2,1,0:T(8,128)(2,1)S(1)} async-done(((bf16[8,96,768]{2,1,0:T(8,128)(2,1)}), bf16[8,96,768]{2,1,0:T(8,128)(2,1)S(1)}, u32[]{:S(2)}, u32[]{:S(2)}) %all-to-all-start.6) | async-done | bytes 1179680 | tf_op jit(solution)/shard_map/all_to_all | solution.py:195
  (679 shorter events, 308.1 us)
Async XLA Ops:
  7.2 84.4 %all-gather.5.cloned.1.call-start = ((), (), s32[]{:S(2)}) async-start(), calls=%async_computation.8 | async-start | bytes 2433024 | tf_op jit(solution)/shard_map/all_gather | solution.py:188
  12.7 101.9 %all-gather.7.cloned.1.call-start = ((), (), s32[]{:S(2)}) async-start(), calls=%async_computation.9 | async-start | bytes 1769472 | tf_op jit(solution)/shard_map/all_gather | solution.py:188
  13.8 143.1 %all-gather.11.cloned.1.call-start = ((), (), s32[]{:S(2)}) async-start(), calls=%async_computation.11 | async-start | bytes 1769472 | tf_op jit(solution)/shard_map/all_gather | solution.py:188
  14.7 193.0 %all-gather.9.cloned.1.call-start = ((), (), s32[]{:S(2)}) async-start(), calls=%async_computation.10 | async-start | bytes 2433024 | tf_op jit(solution)/shard_map/all_gather | solution.py:188
  15.7 57.2 %collective-permute-start = (bf16[256,768]{1,0:T(8,128)(2,1)}, bf16[256,768]{1,0:T(8,128)(2,1)}, u32[]{:S(2)}, u32[]{:S(2)}) collective-permute-start(bf16[256,768]{1,0:T(8,128)(2,1)} %get-tuple-element.170), channel_id=1, source_target_pairs={{0,1},{1,0},{2,3},{3,2},{4,5},{5,4},{6,7},{7,6},{8,9},{9,8},{10,11... | collective-permute-start | bytes 1179656 | tf_op jit(solution)/shard_map/ppermute | solution.py:160
  16.2 58.0 %collective-permute-start.1 = (bf16[256,768]{1,0:T(8,128)(2,1)}, bf16[256,768]{1,0:T(8,128)(2,1)}, u32[]{:S(2)}, u32[]{:S(2)}) collective-permute-start(bf16[256,768]{1,0:T(8,128)(2,1)} %get-tuple-element.170), channel_id=1, source_target_pairs={{0,2},{1,3},{2,0},{3,1},{4,6},{5,7},{6,4},{7,5},{8,10},{9,11},{10,... | collective-permute-start | bytes 1179656 | tf_op jit(solution)/shard_map/ppermute | solution.py:160
  18.8 59.0 %collective-permute-start.10 = (bf16[256,768]{1,0:T(8,128)(2,1)}, bf16[256,768]{1,0:T(8,128)(2,1)}, u32[]{:S(2)}, u32[]{:S(2)}) collective-permute-start(bf16[256,768]{1,0:T(8,128)(2,1)} %get-tuple-element.171), channel_id=1, source_target_pairs={{0,1},{1,0},{2,3},{3,2},{4,5},{5,4},{6,7},{7,6},{8,9},{9,8},{10,11... | collective-permute-start | bytes 1179656 | tf_op jit(solution)/shard_map/ppermute | solution.py:160
  19.0 61.1 %collective-permute-start.11 = (bf16[256,768]{1,0:T(8,128)(2,1)}, bf16[256,768]{1,0:T(8,128)(2,1)}, u32[]{:S(2)}, u32[]{:S(2)}) collective-permute-start(bf16[256,768]{1,0:T(8,128)(2,1)} %get-tuple-element.171), channel_id=1, source_target_pairs={{0,2},{1,3},{2,0},{3,1},{4,6},{5,7},{6,4},{7,5},{8,10},{9,11},{10,... | collective-permute-start | bytes 1179656 | tf_op jit(solution)/shard_map/ppermute | solution.py:160
  20.2 103.2 %collective-permute-start.20 = (bf16[256,768]{1,0:T(8,128)(2,1)}, bf16[256,768]{1,0:T(8,128)(2,1)}, u32[]{:S(2)}, u32[]{:S(2)}) collective-permute-start(bf16[256,768]{1,0:T(8,128)(2,1)} %get-tuple-element.165), channel_id=1, source_target_pairs={{0,1},{1,0},{2,3},{3,2},{4,5},{5,4},{6,7},{7,6},{8,9},{9,8},{10,11... | collective-permute-start | bytes 1179656 | tf_op jit(solution)/shard_map/ppermute | solution.py:160
  72.9 50.0 %collective-permute-start.21 = (bf16[256,768]{1,0:T(8,128)(2,1)}, bf16[256,768]{1,0:T(8,128)(2,1)}, u32[]{:S(2)}, u32[]{:S(2)}) collective-permute-start(bf16[256,768]{1,0:T(8,128)(2,1)} %get-tuple-element.165), channel_id=1, source_target_pairs={{0,2},{1,3},{2,0},{3,1},{4,6},{5,7},{6,4},{7,5},{8,10},{9,11},{10,... | collective-permute-start | bytes 1179656 | tf_op jit(solution)/shard_map/ppermute | solution.py:160
  77.8 49.5 %collective-permute-start.30 = (bf16[256,768]{1,0:T(8,128)(2,1)}, bf16[256,768]{1,0:T(8,128)(2,1)}, u32[]{:S(2)}, u32[]{:S(2)}) collective-permute-start(bf16[256,768]{1,0:T(8,128)(2,1)} %get-tuple-element.166), channel_id=1, source_target_pairs={{0,1},{1,0},{2,3},{3,2},{4,5},{5,4},{6,7},{7,6},{8,9},{9,8},{10,11... | collective-permute-start | bytes 1179656 | tf_op jit(solution)/shard_map/ppermute | solution.py:160
  80.1 47.1 %collective-permute-start.31 = (bf16[256,768]{1,0:T(8,128)(2,1)}, bf16[256,768]{1,0:T(8,128)(2,1)}, u32[]{:S(2)}, u32[]{:S(2)}) collective-permute-start(bf16[256,768]{1,0:T(8,128)(2,1)} %get-tuple-element.166), channel_id=1, source_target_pairs={{0,2},{1,3},{2,0},{3,1},{4,6},{5,7},{6,4},{7,5},{8,10},{9,11},{10,... | collective-permute-start | bytes 1179656 | tf_op jit(solution)/shard_map/ppermute | solution.py:160
  138.6 20.2 %collective-permute-start.6 = (bf16[256,768]{1,0:T(8,128)(2,1)}, bf16[256,768]{1,0:T(8,128)(2,1)}, u32[]{:S(2)}, u32[]{:S(2)}) collective-permute-start(bf16[256,768]{1,0:T(8,128)(2,1)} %get-tuple-element.120), channel_id=1, source_target_pairs={{0,2},{1,3},{2,0},{3,1},{4,6},{5,7},{6,4},{7,5},{8,10},{9,11},{10,... | collective-permute-start | bytes 1179656 | tf_op jit(solution)/shard_map/ppermute | solution.py:160
  140.8 20.4 %collective-permute-start.5 = (bf16[256,768]{1,0:T(8,128)(2,1)}, bf16[256,768]{1,0:T(8,128)(2,1)}, u32[]{:S(2)}, u32[]{:S(2)}) collective-permute-start(bf16[256,768]{1,0:T(8,128)(2,1)} %get-tuple-element.120), channel_id=1, source_target_pairs={{0,1},{1,0},{2,3},{3,2},{4,5},{5,4},{6,7},{7,6},{8,9},{9,8},{10,11... | collective-permute-start | bytes 1179656 | tf_op jit(solution)/shard_map/ppermute | solution.py:160
  252.4 17.7 %collective-permute-start.9 = (bf16[256,768]{1,0:T(8,128)(2,1)S(1)}, bf16[256,768]{1,0:T(8,128)(2,1)S(1)}, u32[]{:S(2)}, u32[]{:S(2)}) collective-permute-start(bf16[256,768]{1,0:T(8,128)(2,1)S(1)} %fusion.125), channel_id=1, source_target_pairs={{0,2},{1,3},{2,0},{3,1},{4,6},{5,7},{6,4},{7,5},{8,10},{9,11},{10,... | collective-permute-start | bytes 1179656 | tf_op jit(solution)/shard_map/ppermute | solution.py:160
  325.6 19.6 %collective-permute-start.28 = (bf16[2,256,768]{2,1,0:T(8,128)(2,1)S(1)}, bf16[2,256,768]{2,1,0:T(8,128)(2,1)S(1)}, u32[]{:S(2)}, u32[]{:S(2)}) collective-permute-start(bf16[2,256,768]{2,1,0:T(8,128)(2,1)S(1)} %dynamic-slice_bitcast_fusion.2), channel_id=1, source_target_pairs={{0,1},{1,0},{2,3},{3,2},{4,5},{5,4},{6,7},{7,6},{8,9},{9,8},{10,11... | collective-permute-start | bytes 2359304 | tf_op jit(solution)/shard_map/ppermute | solution.py:160
  346.2 300.1 %collective-permute-start.29 = (bf16[256,768]{1,0:T(8,128)(2,1)}, bf16[256,768]{1,0:T(8,128)(2,1)}, u32[]{:S(2)}, u32[]{:S(2)}) collective-permute-start(bf16[256,768]{1,0:T(8,128)(2,1)} %fusion.129), channel_id=1, source_target_pairs={{0,2},{1,3},{2,0},{3,1},{4,6},{5,7},{6,4},{7,5},{8,10},{9,11},{10,... | collective-permute-start | bytes 1179656 | tf_op jit(solution)/shard_map/ppermute | solution.py:160
  383.4 37.0 %collective-permute-start.18 = (bf16[2,256,768]{2,1,0:T(8,128)(2,1)}, bf16[2,256,768]{2,1,0:T(8,128)(2,1)}, u32[]{:S(2)}, u32[]{:S(2)}) collective-permute-start(bf16[2,256,768]{2,1,0:T(8,128)(2,1)} %dynamic-slice_bitcast_fusion.4), channel_id=1, source_target_pairs={{0,1},{1,0},{2,3},{3,2},{4,5},{5,4},{6,7},{7,6},{8,9},{9,8},{10,11... | collective-permute-start | bytes 2359304 | tf_op jit(solution)/shard_map/ppermute | solution.py:160
  395.2 22.3 %collective-permute-start.33 = (bf16[2,256,768]{2,1,0:T(8,128)(2,1)}, bf16[2,256,768]{2,1,0:T(8,128)(2,1)}, u32[]{:S(2)}, u32[]{:S(2)}) collective-permute-start(bf16[2,256,768]{2,1,0:T(8,128)(2,1)} %dynamic-slice_bitcast_fusion.1), channel_id=1, source_target_pairs={{0,1},{1,0},{2,3},{3,2},{4,5},{5,4},{6,7},{7,6},{8,9},{9,8},{10,11... | collective-permute-start | bytes 2359304 | tf_op jit(solution)/shard_map/ppermute | solution.py:160
  400.9 25.4 %all-to-all-start.5 = ((bf16[8,96,192]{1,2,0:T(8,128)(2,1)}), bf16[8,96,192]{1,2,0:T(8,128)(2,1)S(1)}, u32[]{:S(2)}, u32[]{:S(2)}) async-start(bf16[8,96,192]{1,2,0:T(8,128)(2,1)} %copy.124), calls=%async_computation.5 | async-start | bytes 786432 | tf_op jit(solution)/shard_map/all_to_all | solution.py:195
  424.9 15.0 %collective-permute-start.19 = (bf16[256,768]{1,0:T(8,128)(2,1)}, bf16[256,768]{1,0:T(8,128)(2,1)}, u32[]{:S(2)}, u32[]{:S(2)}) collective-permute-start(bf16[256,768]{1,0:T(8,128)(2,1)} %fusion.127), channel_id=1, source_target_pairs={{0,2},{1,3},{2,0},{3,1},{4,6},{5,7},{6,4},{7,5},{8,10},{9,11},{10,... | collective-permute-start | bytes 1179656 | tf_op jit(solution)/shard_map/ppermute | solution.py:160
  426.3 64.4 %all-to-all-start.2 = ((bf16[8,96,576]{2,1,0:T(8,128)(2,1)}), bf16[8,96,576]{2,1,0:T(8,128)(2,1)}, u32[]{:S(2)}, u32[]{:S(2)}) async-start(bf16[8,96,576]{2,1,0:T(8,128)(2,1)} %bitcast.414), calls=%async_computation.2 | async-start | bytes 1966080 | tf_op jit(solution)/shard_map/all_to_all | solution.py:195
  444.1 46.6 %collective-permute-start.36 = (bf16[256,768]{1,0:T(8,128)(2,1)}, bf16[256,768]{1,0:T(8,128)(2,1)}, u32[]{:S(2)}, u32[]{:S(2)}) collective-permute-start(bf16[256,768]{1,0:T(8,128)(2,1)} %get-tuple-element.118), channel_id=1, source_target_pairs={{0,2},{1,3},{2,0},{3,1},{4,6},{5,7},{6,4},{7,5},{8,10},{9,11},{10,... | collective-permute-start | bytes 1179656 | tf_op jit(solution)/shard_map/ppermute | solution.py:160
  445.4 51.5 %collective-permute-start.35 = (bf16[256,768]{1,0:T(8,128)(2,1)}, bf16[256,768]{1,0:T(8,128)(2,1)S(1)}, u32[]{:S(2)}, u32[]{:S(2)}) collective-permute-start(bf16[256,768]{1,0:T(8,128)(2,1)} %get-tuple-element.118), channel_id=1, source_target_pairs={{0,1},{1,0},{2,3},{3,2},{4,5},{5,4},{6,7},{7,6},{8,9},{9,8},{10,11... | collective-permute-start | bytes 1179656 | tf_op jit(solution)/shard_map/ppermute | solution.py:160
  490.7 79.8 %all-to-all-start.7 = ((bf16[8,96,768]{2,1,0:T(8,128)(2,1)}), bf16[8,96,768]{2,1,0:T(8,128)(2,1)}, u32[]{:S(2)}, u32[]{:S(2)}) async-start(bf16[8,96,768]{2,1,0:T(8,128)(2,1)} %bitcast.424), calls=%async_computation.7 | async-start | bytes 2359296 | tf_op jit(solution)/shard_map/all_to_all | solution.py:195
  570.6 26.2 %all-to-all-start.3 = ((bf16[8,96,768]{2,1,0:T(8,128)(2,1)}), bf16[8,96,768]{2,1,0:T(8,128)(2,1)}, u32[]{:S(2)}, u32[]{:S(2)}) async-start(bf16[8,96,768]{2,1,0:T(8,128)(2,1)} %bitcast.423), calls=%async_computation.3 | async-start | bytes 2359296 | tf_op jit(solution)/shard_map/all_to_all | solution.py:195
  587.9 36.1 %collective-permute-start.38 = (bf16[2,256,768]{2,1,0:T(8,128)(2,1)}, bf16[2,256,768]{2,1,0:T(8,128)(2,1)}, u32[]{:S(2)}, u32[]{:S(2)}) collective-permute-start(bf16[2,256,768]{2,1,0:T(8,128)(2,1)} %dynamic-slice_bitcast_fusion), channel_id=1, source_target_pairs={{0,1},{1,0},{2,3},{3,2},{4,5},{5,4},{6,7},{7,6},{8,9},{9,8},{10,11... | collective-permute-start | bytes 2359304 | tf_op jit(solution)/shard_map/ppermute | solution.py:160
  596.7 14.5 %all-to-all-start.4 = ((bf16[8,96,192]{1,2,0:T(8,128)(2,1)}), bf16[8,96,192]{1,2,0:T(8,128)(2,1)S(1)}, u32[]{:S(2)}, u32[]{:S(2)}) async-start(bf16[8,96,192]{1,2,0:T(8,128)(2,1)} %copy.123), calls=%async_computation.4 | async-start | bytes 786432 | tf_op jit(solution)/shard_map/all_to_all | solution.py:195
  611.2 27.8 %all-to-all-start = ((bf16[8,96,576]{2,1,0:T(8,128)(2,1)}), bf16[8,96,576]{2,1,0:T(8,128)(2,1)}, u32[]{:S(2)}, u32[]{:S(2)}) async-start(bf16[8,96,576]{2,1,0:T(8,128)(2,1)} %bitcast.79), calls=%async_computation | async-start | bytes 1966080 | tf_op jit(solution)/shard_map/all_to_all | solution.py:195
  626.1 19.7 %collective-permute-start.39 = (bf16[256,768]{1,0:T(8,128)(2,1)}, bf16[256,768]{1,0:T(8,128)(2,1)S(1)}, u32[]{:S(2)}, u32[]{:S(2)}) collective-permute-start(bf16[256,768]{1,0:T(8,128)(2,1)} %fusion.131), channel_id=1, source_target_pairs={{0,2},{1,3},{2,0},{3,1},{4,6},{5,7},{6,4},{7,5},{8,10},{9,11},{10,... | collective-permute-start | bytes 1179656 | tf_op jit(solution)/shard_map/ppermute | solution.py:160
  639.0 32.2 %all-to-all-start.1 = ((bf16[8,96,768]{2,1,0:T(8,128)(2,1)}), bf16[8,96,768]{2,1,0:T(8,128)(2,1)S(1)}, u32[]{:S(2)}, u32[]{:S(2)}) async-start(bf16[8,96,768]{2,1,0:T(8,128)(2,1)} %bitcast.426), calls=%async_computation.1 | async-start | bytes 2359296 | tf_op jit(solution)/shard_map/all_to_all | solution.py:195
  671.2 32.4 %all-to-all-start.6 = ((bf16[8,96,768]{2,1,0:T(8,128)(2,1)}), bf16[8,96,768]{2,1,0:T(8,128)(2,1)S(1)}, u32[]{:S(2)}, u32[]{:S(2)}) async-start(bf16[8,96,768]{2,1,0:T(8,128)(2,1)} %bitcast.425), calls=%async_computation.6 | async-start | bytes 2359296 | tf_op jit(solution)/shard_map/all_to_all | solution.py:195
  (166 other events, 1566.8 us)
Sparse Core Ops, SparseCore 0:
  12.9 53.2 all-gather.4
  68.9 42.7 all-gather.6
  113.9 42.9 all-gather.10
  158.9 48.7 all-gather.8
